TPU v7x, 32 devices: a whole 2x2x4 slice. The times are simulated.
32 devices in a mesh: groups: 2 (over y), blk: 4 (over z), heads: 2 (over x), sub: 2 (over core).
Axes of the slice: x: 2, y: 2, z: 4, core: 2. Of those that a mesh axis runs over, the one named last changes fastest.
Arguments:
- patches: bfloat16 [1024, 1024], P(('groups', 'blk')), parts along dimension 0, may hold values from -6 to 6
- conv_taps: float32 [3, 1024], replicated, may hold values from -3 to 3
- w_query: bfloat16 [1024, 1024], P(None, ('heads', 'sub')), may hold values from -0.1875 to 0.1875
- w_key: bfloat16 [1024, 1024], P(None, ('heads', 'sub')), may hold values from -0.1875 to 0.1875
- w_value: bfloat16 [1024, 1024], P(None, ('heads', 'sub')), may hold values from -0.1875 to 0.1875
- w_output: bfloat16 [1024, 1024], P(None, ('heads', 'sub')), may hold values from -0.1875 to 0.1875
- tile_mask: int32 [8, 4], P('groups'), parts along dimension 0, may hold values from 0 to 1, as said below
- cotangent: bfloat16 [1024, 1024], P(('groups', 'blk'), ('heads', 'sub')), parts along dimension 0, may hold values from -6 to 6
Outputs:
- input_grad: float32 [1024, 1024], P(('groups', 'blk'), ('heads', 'sub')), parts along dimension 0
- conv_grad: float32 [6, 1024], P('groups', ('heads', 'sub')), parts along dimension 0
- grad_query: float32 [2048, 1024], P(('groups', 'blk'), ('heads', 'sub')), parts along dimension 0
- grad_key: float32 [2048, 1024], P(('groups', 'blk'), ('heads', 'sub')), parts along dimension 0
- grad_value: float32 [2048, 1024], P(('groups', 'blk'), ('heads', 'sub')), parts along dimension 0
- grad_output: float32 [2048, 1024], P(('groups', 'blk'), ('heads', 'sub')), parts along dimension 0
There are 2 independent parts, one for each index of `groups`. A program takes and returns all parts, laid end to end along the dimension named above; an argument that names none is the same for every part. Nothing has to cross between parts.
Inputs may be any that keep to these rules, and one draw needn't show every extreme that they name: tile_mask[i][i] is 1 for every tile and tile_mask is symmetric.
All inputs are finite; a program needn't handle non-finite values.
Results may differ from a plain program's by a relative error of at most 0.004.
The roundings to bfloat16 on the way count: a program that leaves them out, or rounds other values in their place, can miss the bound.
Values may be sent and summed in bfloat16 or wider, within the bound.
A program may use at most 64 MiB of HBM per device.

v0:
```python
import jax
import jax.numpy as jnp
from jax import lax
from jax.sharding import PartitionSpec as P

D = 1024
HEADS = 16
TILE = 128


def padded(cells, sides, width):
    for axis, dim in sides:
        count = lax.axis_size(axis)
        ends = count - 1
        head = lax.slice_in_dim(cells, 0, width, axis=dim)
        tail = lax.slice_in_dim(cells, cells.shape[dim] - width, cells.shape[dim], axis=dim)
        cells = jnp.concatenate(
            [
                lax.ppermute(tail, axis, [(i, (i + 1) % count) for i in range(ends)]),
                cells,
                lax.ppermute(head, axis, [((i + 1) % count, i) for i in range(ends)]),
            ],
            axis=dim,
        )
    return cells


def from_behind(value, axis, steps):
    count = lax.axis_size(axis)
    pairs = [(source, (source + steps) % count) for source in range(count)]
    return lax.ppermute(value, axis, pairs)


def allowed_rows(mask_bf, first_query, query_count, first_key, key_count):
    tiles = mask_bf.shape[0]
    columns = jnp.arange(tiles, dtype=jnp.int32)
    query_tiles = (first_query + jnp.arange(query_count, dtype=jnp.int32)) // TILE
    key_tiles = (first_key + jnp.arange(key_count, dtype=jnp.int32)) // TILE
    query_hot = (query_tiles[:, None] == columns[None, :]).astype(jnp.bfloat16)
    key_hot = (key_tiles[:, None] == columns[None, :]).astype(jnp.bfloat16)
    picked = jnp.dot(query_hot, mask_bf, preferred_element_type=jnp.float32).astype(jnp.bfloat16)
    return jnp.einsum("qn,kn->qk", picked, key_hot, preferred_element_type=jnp.float32) > 0.5


def per_device(patches, conv_taps, w_query, w_key, w_value, w_output, tile_mask, cotangent):
    rows = patches.shape[0]
    local = w_query.shape[1]
    head_size = D // HEADS
    heads_here = local // head_size
    cycle_size = lax.axis_size("blk")
    position = lax.axis_index("blk")
    total_rows = rows * cycle_size
    scale = head_size ** (-0.5)
    norm = total_rows ** (-0.5)
    mask_bf = tile_mask.astype(jnp.bfloat16)
    first_query = position * rows
    padded_in = padded(patches, (("blk", 0),), 1)
    padded32 = padded_in.astype(jnp.float32)
    middle = padded32[1:-1]
    mixed = (
        middle + conv_taps[0] * padded32[:-2] + conv_taps[1] * middle + conv_taps[2] * padded32[2:]
    ).astype(jnp.bfloat16)
    queries = jnp.dot(mixed, w_query, preferred_element_type=jnp.float32).astype(jnp.bfloat16)
    keys_own = jnp.dot(mixed, w_key, preferred_element_type=jnp.float32).astype(jnp.bfloat16)
    values_own = jnp.dot(mixed, w_value, preferred_element_type=jnp.float32).astype(jnp.bfloat16)
    keys_all, values_all = (
        lax.all_gather(keys_own, "blk", axis=0, tiled=True),
        lax.all_gather(values_own, "blk", axis=0, tiled=True),
    )
    cot_full = lax.all_gather(cotangent, ("heads", "sub"), axis=1, tiled=True)
    grad_att = jnp.dot(cot_full, w_output, preferred_element_type=jnp.float32).astype(jnp.bfloat16)
    group = 1
    for power in range(12):
        if group * 2 * rows <= 1024 and cycle_size % (group * 2) == 0:
            group = group * 2
    span = group * rows
    blocks = cycle_size // group
    query_heads = queries.reshape(rows, heads_here, head_size)
    grad_heads = grad_att.reshape(rows, heads_here, head_size)
    key_blocks = keys_all.reshape(blocks, span, heads_here, head_size)
    value_blocks = values_all.reshape(blocks, span, heads_here, head_size)
    block_ids = jnp.arange(blocks, dtype=jnp.int32)

    def weights_of(key_block, allowed):
        raw = (
            jnp.einsum("qhd,khd->hqk", query_heads, key_block, preferred_element_type=jnp.float32)
            * scale
        )
        return jnp.where(allowed[None], jnp.exp(jnp.where(allowed[None], raw, 0.0)), 0.0)

    def forward_step(state, inputs):
        block_id, key_block, value_block = inputs
        allowed = allowed_rows(mask_bf, first_query, rows, block_id * span, span)
        accum, totals = state
        weights = weights_of(key_block, allowed)
        added = jnp.einsum(
            "hqk,khd->hqd",
            weights.astype(jnp.bfloat16),
            value_block,
            preferred_element_type=jnp.float32,
        )
        state = (accum + added, totals + jnp.sum(weights, -1))
        return (state, None)

    start_state = (
        jnp.zeros((heads_here, rows, head_size), jnp.float32),
        jnp.zeros((heads_here, rows), jnp.float32),
    )
    (accum, totals), unused = lax.scan(
        forward_step, start_state, (block_ids, key_blocks, value_blocks)
    )
    attended32 = accum / totals[:, :, None]
    attended = jnp.transpose(attended32, (1, 0, 2)).reshape(rows, local).astype(jnp.bfloat16)
    deltas = jnp.einsum("qhd,hqd->hq", grad_heads.astype(jnp.float32), attended32)

    def local_grads(key_block, value_block, allowed):
        weights = weights_of(key_block, allowed)
        probs = weights / totals[:, :, None]
        dprobs = jnp.einsum(
            "qhd,khd->hqk", grad_heads, value_block, preferred_element_type=jnp.float32
        )
        dscores = (probs * (dprobs - deltas[:, :, None]) * scale).astype(jnp.bfloat16)
        return (
            jnp.einsum("hqk,khd->qhd", dscores, key_block, preferred_element_type=jnp.float32),
            jnp.einsum("hqk,qhd->khd", dscores, query_heads, preferred_element_type=jnp.float32),
            jnp.einsum(
                "hqk,qhd->khd",
                probs.astype(jnp.bfloat16),
                grad_heads,
                preferred_element_type=jnp.float32,
            ),
        )

    def shard_grads(block):
        wrapped = jnp.remainder(block, cycle_size)
        key_block = lax.dynamic_slice_in_dim(keys_all, wrapped * rows, rows, 0).reshape(
            rows, heads_here, head_size
        )
        value_block = lax.dynamic_slice_in_dim(values_all, wrapped * rows, rows, 0).reshape(
            rows, heads_here, head_size
        )
        allowed = allowed_rows(mask_bf, first_query, rows, wrapped * rows, rows)
        query_add, key_term, value_term = local_grads(key_block, value_block, allowed)
        return (
            query_add,
            jnp.stack([key_term.reshape(rows, local), value_term.reshape(rows, local)]),
        )

    query_first, carried_first = shard_grads(position - 1)

    def turn(step, state):
        accum_q, carried = state
        moved = from_behind(carried, "blk", 1)
        query_add, term = shard_grads(position - step - 1)
        return (accum_q + query_add, moved + term)

    accum_q, summed = lax.fori_loop(1, cycle_size, turn, (query_first, carried_first))
    grad_keys = summed[0].astype(jnp.bfloat16)
    grad_values = summed[1].astype(jnp.bfloat16)
    grad_queries = accum_q.reshape(rows, local).astype(jnp.bfloat16)
    stacked = jnp.stack(
        [
            jnp.einsum("td,tc->dc", mixed, grad_queries, preferred_element_type=jnp.float32),
            jnp.einsum("td,tc->dc", mixed, grad_keys, preferred_element_type=jnp.float32),
            jnp.einsum("td,tc->dc", mixed, grad_values, preferred_element_type=jnp.float32),
            jnp.einsum("td,tc->dc", cot_full, attended, preferred_element_type=jnp.float32),
        ]
    )
    weight_sums = lax.psum_scatter(stacked, "blk", scatter_dimension=1, tiled=True) * norm
    partial_grad = (
        jnp.einsum("tc,dc->td", grad_queries, w_query, preferred_element_type=jnp.float32)
        + jnp.einsum("tc,dc->td", grad_keys, w_key, preferred_element_type=jnp.float32)
        + jnp.einsum("tc,dc->td", grad_values, w_value, preferred_element_type=jnp.float32)
    )
    grad_mixed = lax.psum_scatter(
        partial_grad, ("heads", "sub"), scatter_dimension=1, tiled=True
    ) + cotangent.astype(jnp.float32)
    columns_here = cotangent.shape[1]
    offset = lax.axis_index(("heads", "sub")) * columns_here
    taps_here = lax.dynamic_slice_in_dim(conv_taps, offset, columns_here, 1)
    padded_grad = padded(grad_mixed.astype(jnp.bfloat16), (("blk", 0),), 1).astype(grad_mixed.dtype)
    input_grad = (
        grad_mixed * (1.0 + taps_here[1])
        + taps_here[0] * padded_grad[2:]
        + taps_here[2] * padded_grad[:-2]
    )
    patch_cols = lax.dynamic_slice_in_dim(padded32, offset, columns_here, 1)
    conv_terms = jnp.stack(
        [
            jnp.sum(grad_mixed * patch_cols[:-2], 0),
            jnp.sum(grad_mixed * patch_cols[1:-1], 0),
            jnp.sum(grad_mixed * patch_cols[2:], 0),
        ]
    )
    conv_grad = lax.psum(conv_terms, "blk") * norm
    return (input_grad, conv_grad, weight_sums[0], weight_sums[1], weight_sums[2], weight_sums[3])


def solution(mesh):
    in_specs = (
        P(("groups", "blk"), None),
        P(),
        P(None, ("heads", "sub")),
        P(None, ("heads", "sub")),
        P(None, ("heads", "sub")),
        P(None, ("heads", "sub")),
        P("groups", None),
        P(("groups", "blk"), ("heads", "sub")),
    )
    out_specs = (
        P(("groups", "blk"), ("heads", "sub")),
        P("groups", ("heads", "sub")),
        P(("groups", "blk"), ("heads", "sub")),
        P(("groups", "blk"), ("heads", "sub")),
        P(("groups", "blk"), ("heads", "sub")),
        P(("groups", "blk"), ("heads", "sub")),
    )
    return jax.shard_map(
        per_device, mesh=mesh, in_specs=in_specs, out_specs=out_specs, check_vma=False
    )
```

profile of v0, /device:TPU:0, one launch (start us, length us, event | category | flops | bytes accessed | tf_op | source)
XLA Modules:
  0.0 201.9 jit_solution(833007776584470410)
XLA Ops:
  7.2 0.9 fusion.47
  8.1 4.9 %collective-permute-start.1 = (bf16[1,1024]{1,0:T(2,128)(2,1)S(1)}, bf16[1,1024]{1,0:T(2,128)(2,1)S(1)}, u32[]{:S(2)}, u32[]{:S(2)}) collective-permute-start(bf16[1,1024]{1,0:T(2,128)(2,1)S(1)} %get-tuple-element.416), channel_id=1, source_target_pairs={{0,4},{4,8},{8,12},{1,5},{5,9},{9,13},{2,6},{6,10},{10,14},{3,7},{... | collective-permute-start | bytes 6152 | tf_op jit(solution)/shard_map/ppermute | solution.py:19
  13.0 1.3 collective-permute-start.2
  15.9 6.0 %all_gather.10 = bf16[128,1024]{1,0:T(8,128)(2,1)S(1)} all-gather(bf16[128,256]{1,0:T(8,128)(2,1)} %param.17), channel_id=1, replica_groups=mesh['groups'=2,'blk'=4,'heads'=2,'sub'=2] {'heads','sub'}, dimensions={1}, use_global_device_ids=true | all-gather | bytes 327680 | tf_op jit(solution)/shard_map/all_gather | solution.py:70
  22.5 1.3 convolution_convert_fusion.2
  24.2 1.0 maximum_convert_fusion
  26.3 15.2 %all_gather.9 = bf16[512,256]{1,0:T(8,128)(2,1)S(1)} all-gather(bf16[128,256]{1,0:T(8,128)(2,1)S(1)} %convolution_convert_fusion.4), channel_id=1, replica_groups=mesh['groups'=2,'blk'=4,'heads'=2,'sub'=2] {'blk'}, dimensions={0}, use_global_device_ids=true | all-gather | bytes 327680 | tf_op jit(solution)/shard_map/all_gather | solution.py:67
  41.4 14.4 %all_gather.11 = bf16[512,256]{1,0:T(8,128)(2,1)S(1)} all-gather(bf16[128,256]{1,0:T(8,128)(2,1)S(1)} %convolution_convert_fusion.1), channel_id=1, replica_groups=mesh['groups'=2,'blk'=4,'heads'=2,'sub'=2] {'blk'}, dimensions={0}, use_global_device_ids=true | all-gather | bytes 327680 | tf_op jit(solution)/shard_map/all_gather | solution.py:68
  55.9 0.8 copy.38
  57.8 1.5 fusion.50
  59.6 1.9 fusion.37
  62.3 29.1 %while.23 = (s32[]{:T(128)}, f32[128,4,64]{0,2,1:T(8,128)S(1)}, f32[2,128,256]{1,2,0:T(8,128)S(1)}, s32[]{:T(128)}, bf16[512,256]{0,1:T(8,128)(2,1)}, /*index=5*...) while((s32[]{:T(128)}, f32[128,4,64]{0,2,1:T(8,128)S(1)}, ...), condition=%wide.region_2.3_spmd, body=%wide.region_1.2_spmd.sunk | while | flops 42853904 | bytes 4331956 | solution.py:157
  62.3 1.6 collective-permute-start
  64.5 0.9 constant_dynamic-slice_fusion.6
  66.5 5.7 %collective-permute-done = f32[2,128,256]{1,2,0:T(8,128)S(1)} collective-permute-done((f32[2,128,256]{1,2,0:T(8,128)S(1)}, f32[2,128,256]{1,2,0:T(8,128)S(1)}, u32[]{:S(2)}, u32[]{:S(2)}) %collective-permute-start) | collective-permute-done | bytes 262176 | tf_op jit(solution)/shard_map/while/body/eval_jaxpr/ppermute | solution.py:31
  72.2 1.0 collective-permute-start
  73.7 0.9 constant_dynamic-slice_fusion.6
  75.6 7.4 %collective-permute-done = f32[2,128,256]{1,2,0:T(8,128)S(1)} collective-permute-done((f32[2,128,256]{1,2,0:T(8,128)S(1)}, f32[2,128,256]{1,2,0:T(8,128)S(1)}, u32[]{:S(2)}, u32[]{:S(2)}) %collective-permute-start) | collective-permute-done | bytes 262176 | tf_op jit(solution)/shard_map/while/body/eval_jaxpr/ppermute | solution.py:31
  83.7 0.9 constant_dynamic-slice_fusion.6
  85.7 5.7 %collective-permute-done = f32[2,128,256]{1,2,0:T(8,128)S(1)} collective-permute-done((f32[2,128,256]{1,2,0:T(8,128)S(1)}, f32[2,128,256]{1,2,0:T(8,128)S(1)}, u32[]{:S(2)}, u32[]{:S(2)}) %collective-permute-start) | collective-permute-done | bytes 262176 | tf_op jit(solution)/shard_map/while/body/eval_jaxpr/ppermute | solution.py:31
  92.1 1.1 convolution_add_fusion
  94.6 2.2 %pad_maximum_fusion = f32[4,1024,256]{2,1,0:T(8,128)} fusion(f32[1,1024,256]{2,1,0:T(8,128)S(1)} %convolution_bitcast_fusion.1, f32[1,1024,256]{2,1,0:T(8,128)S(1)} %convolution_bitcast_fusion.2, f32[1,1024,256]{2,1,0:T(8,128)S(1)} %convolution_bitcast_fusion.3, f32[1,1024,256]{2,1,0:T(8,128)S(1)} %convolution_bitcast_fusion.4), kind=kLoop, calls=%fused_computation.32 | loop fusion | flops 3145728 | bytes 8388608 | tf_op jit(solution)/shard_map/stack | solution.py:161
  96.9 0.9 dynamic-slice_add_fusion
  97.8 15.5 %reduce-scatter.3.cloned.1.call-done = f32[128,256]{1,0:T(8,128)} async-done(((f32[128,1024]{1,0:T(8,128)}), f32[128,256]{1,0:T(8,128)}) %reduce-scatter.3.cloned.1.call-update) | async-done | bytes 131088 | tf_op jit(solution)/shard_map/reduce_scatter | solution.py:175
  113.3 1.1 fusion.33
  114.3 3.4 %collective-permute-start.3 = (bf16[1,256]{1,0:T(2,128)(2,1)S(1)}, bf16[1,256]{1,0:T(2,128)(2,1)S(1)}, u32[]{:S(2)}, u32[]{:S(2)}) collective-permute-start(bf16[1,256]{1,0:T(2,128)(2,1)S(1)} %get-tuple-element.419), channel_id=1, source_target_pairs={{0,4},{4,8},{8,12},{1,5},{5,9},{9,13},{2,6},{6,10},{10,14},{3,7},{... | collective-permute-start | bytes 1544 | tf_op jit(solution)/shard_map/ppermute | solution.py:19
  117.7 1.3 collective-permute-start.4
  119.1 13.3 %psum.7 = f32[3,256]{1,0:T(4,128)S(1)} all-reduce(f32[3,256]{1,0:T(4,128)S(1)} %pad_maximum_fusion.2), channel_id=1, replica_groups=mesh['groups'=2,'blk'=4,'heads'=2,'sub'=2] {'blk'}, use_global_device_ids=true, to_apply=%region_7.8 | all-reduce | flops 768 | bytes 6144 | tf_op jit(solution)/shard_map/psum | solution.py:195
  133.0 1.6 fusion.34
  134.6 58.2 %reduce-scatter.5.cloned.1.call-done = f32[4,256,256]{2,1,0:T(8,128)} async-done(((f32[4,1024,256]{2,1,0:T(8,128)}), f32[4,256,256]{2,1,0:T(8,128)}) %reduce-scatter.5.cloned.1.call-update) | async-done | bytes 1048592 | tf_op jit(solution)/shard_map/reduce_scatter | solution.py:169
  192.7 1.3 broadcast_multiply_fusion
  194.1 1.0 slice_bitcast_fusion
  (86 shorter events, 13.0 us)
Async XLA Ops:
  7.2 18.5 %copy-start = (bf16[1024,256]{1,0:T(8,128)(2,1)S(1)}, bf16[1024,256]{1,0:T(8,128)(2,1)}, u32[]{:S(2)}) copy-start(bf16[1024,256]{1,0:T(8,128)(2,1)} %param.12) | copy-start | bytes 1572868
  7.2 18.2 %copy-start.2 = (bf16[1024,256]{1,0:T(8,128)(2,1)S(1)}, bf16[1024,256]{1,0:T(8,128)(2,1)}, u32[]{:S(2)}) copy-start(bf16[1024,256]{1,0:T(8,128)(2,1)} %param.14) | copy-start | bytes 1572868
  7.2 18.8 %copy-start.1 = (bf16[1024,256]{1,0:T(8,128)(2,1)S(1)}, bf16[1024,256]{1,0:T(8,128)(2,1)}, u32[]{:S(2)}) copy-start(bf16[1024,256]{1,0:T(8,128)(2,1)} %param.13) | copy-start | bytes 1572868
  7.2 106.1 %reduce-scatter.3.cloned.1.call-start = ((), (), s32[]{:S(2)}) async-start(), calls=%async_computation.2 | async-start | bytes 655360 | tf_op jit(solution)/shard_map/reduce_scatter | solution.py:175
  8.1 16.1 %collective-permute-start.1 = (bf16[1,1024]{1,0:T(2,128)(2,1)S(1)}, bf16[1,1024]{1,0:T(2,128)(2,1)S(1)}, u32[]{:S(2)}, u32[]{:S(2)}) collective-permute-start(bf16[1,1024]{1,0:T(2,128)(2,1)S(1)} %get-tuple-element.416), channel_id=1, source_target_pairs={{0,4},{4,8},{8,12},{1,5},{5,9},{9,13},{2,6},{6,10},{10,14},{3,7},{... | collective-permute-start | bytes 6152 | tf_op jit(solution)/shard_map/ppermute | solution.py:19
  13.0 11.1 %collective-permute-start.2 = (bf16[1,1024]{1,0:T(2,128)(2,1)S(1)}, bf16[1,1024]{1,0:T(2,128)(2,1)S(1)}, u32[]{:S(2)}, u32[]{:S(2)}) collective-permute-start(bf16[1,1024]{1,0:T(2,128)(2,1)S(1)} %get-tuple-element.417), channel_id=1, source_target_pairs={{4,0},{8,4},{12,8},{5,1},{9,5},{13,9},{6,2},{10,6},{14,10},{7,3},{... | collective-permute-start | bytes 6152 | tf_op jit(solution)/shard_map/ppermute | solution.py:21
  62.3 9.8 %collective-permute-start = (f32[2,128,256]{1,2,0:T(8,128)S(1)}, f32[2,128,256]{1,2,0:T(8,128)S(1)}, u32[]{:S(2)}, u32[]{:S(2)}) collective-permute-start(f32[2,128,256]{1,2,0:T(8,128)S(1)} %get-tuple-element.533), channel_id=1, source_target_pairs={{0,4},{4,8},{8,12},{12,0},{1,5},{5,9},{9,13},{13,1},{2,6},{6,10},{... | collective-permute-start | bytes 786440 | tf_op jit(solution)/shard_map/while/body/eval_jaxpr/ppermute | solution.py:31
  72.2 10.9 %collective-permute-start = (f32[2,128,256]{1,2,0:T(8,128)S(1)}, f32[2,128,256]{1,2,0:T(8,128)S(1)}, u32[]{:S(2)}, u32[]{:S(2)}) collective-permute-start(f32[2,128,256]{1,2,0:T(8,128)S(1)} %get-tuple-element.533), channel_id=1, source_target_pairs={{0,4},{4,8},{8,12},{12,0},{1,5},{5,9},{9,13},{13,1},{2,6},{6,10},{... | collective-permute-start | bytes 786440 | tf_op jit(solution)/shard_map/while/body/eval_jaxpr/ppermute | solution.py:31
  83.1 8.2 %collective-permute-start = (f32[2,128,256]{1,2,0:T(8,128)S(1)}, f32[2,128,256]{1,2,0:T(8,128)S(1)}, u32[]{:S(2)}, u32[]{:S(2)}) collective-permute-start(f32[2,128,256]{1,2,0:T(8,128)S(1)} %get-tuple-element.533), channel_id=1, source_target_pairs={{0,4},{4,8},{8,12},{12,0},{1,5},{5,9},{9,13},{13,1},{2,6},{6,10},{... | collective-permute-start | bytes 786440 | tf_op jit(solution)/shard_map/while/body/eval_jaxpr/ppermute | solution.py:31
  91.7 2.5 %copy-start.4 = (f32[4,128,64]{1,2,0:T(8,128)S(1)}, f32[4,128,64]{1,2,0:T(8,128)}, u32[]{:S(2)}) copy-start(f32[4,128,64]{1,2,0:T(8,128)} %get-tuple-element.430) | copy-start | bytes 393220
  93.2 99.5 %reduce-scatter.5.cloned.1.call-start = ((), (), s32[]{:S(2)}) async-start(), calls=%async_computation.3 | async-start | bytes 5242880 | tf_op jit(solution)/shard_map/reduce_scatter | solution.py:169
  96.9 16.4 %copy-start.3 = (bf16[128,256]{1,0:T(8,128)(2,1)S(1)}, bf16[128,256]{1,0:T(8,128)(2,1)}, u32[]{:S(2)}) copy-start(bf16[128,256]{1,0:T(8,128)(2,1)} %param.17) | copy-start | bytes 196612
  114.3 18.6 %collective-permute-start.3 = (bf16[1,256]{1,0:T(2,128)(2,1)S(1)}, bf16[1,256]{1,0:T(2,128)(2,1)S(1)}, u32[]{:S(2)}, u32[]{:S(2)}) collective-permute-start(bf16[1,256]{1,0:T(2,128)(2,1)S(1)} %get-tuple-element.419), channel_id=1, source_target_pairs={{0,4},{4,8},{8,12},{1,5},{5,9},{9,13},{2,6},{6,10},{10,14},{3,7},{... | collective-permute-start | bytes 1544 | tf_op jit(solution)/shard_map/ppermute | solution.py:19
  117.7 15.2 %collective-permute-start.4 = (bf16[1,256]{1,0:T(2,128)(2,1)S(1)}, bf16[1,256]{1,0:T(2,128)(2,1)S(1)}, u32[]{:S(2)}, u32[]{:S(2)}) collective-permute-start(bf16[1,256]{1,0:T(2,128)(2,1)S(1)} %get-tuple-element.420), channel_id=1, source_target_pairs={{4,0},{8,4},{12,8},{5,1},{9,5},{13,9},{6,2},{10,6},{14,10},{7,3},{... | collective-permute-start | bytes 1544 | tf_op jit(solution)/shard_map/ppermute | solution.py:21
Sparse Core Ops, SparseCore 0:
  93.4 19.8 reduce-scatter.2
  115.7 77.0 reduce-scatter.4
where the time goes:
time: 203 us; the launch traced here: 202 us
  waiting for transfers between devices  92.5 us (46%)
  blocking collectives  48.9 us (24%)
  matrix products  14.4 us (7%)
  between operations  14.4 us (7%)
  starting transfers between devices  13.7 us (7%)
  other arithmetic  9.88 us (5%)
  local copies, waits for them, and re-layouts  7.87 us (4%)
    reduce_scatter x1, waiting for transfers between devices, per_device(): lax.psum_scatter(stacked, 'blk', scatter_dimension=1, tiled=True) * norm  58.2 us
    ppermute x3, waiting for transfers between devices, from_behind(): return lax.ppermute(value, axis, pairs)  18.8 us
    reduce_scatter x1, waiting for transfers between devices, per_device(): lax.psum_scatter(partial_grad, ('heads', 'sub'), scatter_dimension=1, til...  15.5 us
    all_gather x1, blocking collectives, per_device(): lax.all_gather(keys_own, 'blk', axis=0, tiled=True)  15.2 us
    all_gather x1, blocking collectives, per_device(): lax.all_gather(values_own, 'blk', axis=0, tiled=True)  14.4 us
    psum x1, blocking collectives, per_device(): conv_grad = lax.psum(conv_terms, 'blk') * norm  13.3 us
    ppermute x2, starting transfers between devices, padded(): lax.ppermute(tail, axis, [(i, (i + 1) % count) for i in range(ends)])  8.32 us
    all_gather x1, blocking collectives, per_device(): cot_full = lax.all_gather(cotangent, ('heads', 'sub'), axis=1, tiled=True)  6 us
  transfers between devices with their start and end apart: 9, of which 5 were waited for; matrix products, arithmetic and copies ran while one was open for 9% of the time, Pallas kernels for 0%

commit v1 on v0

--- a/solution.py
+++ b/solution.py
@@ -6,6 +6,22 @@
 D = 1024
 HEADS = 16
 TILE = 128
+
+
+def plate_manage(chunk, along_axis="blk"):
+    n_dev_all = lax.axis_size(along_axis)
+    seen = [(q, (q + 1) % n_dev_all) for q in range(n_dev_all)]
+    lanes = [(q, (q - 1) % n_dev_all) for q in range(n_dev_all)]
+    w1, e_next = ([chunk], [chunk])
+    for _ in range(n_dev_all // 2):
+        aux = lax.ppermute(w1[-1], along_axis, seen)
+        w1.append(aux)
+    for _ in range((n_dev_all - 1) // 2):
+        piece_out = lax.ppermute(e_next[-1], along_axis, lanes)
+        e_next.append(piece_out)
+    parts_out = jnp.concatenate([*w1[::-1], *e_next[1:]], axis=0)
+    before = lax.axis_index(along_axis)
+    return jnp.roll(parts_out, (before - n_dev_all // 2) * chunk.shape[0], 0)
 
 
 def padded(cells, sides, width):
@@ -65,7 +81,7 @@
     values_own = jnp.dot(mixed, w_value, preferred_element_type=jnp.float32).astype(jnp.bfloat16)
     keys_all, values_all = (
         lax.all_gather(keys_own, "blk", axis=0, tiled=True),
-        lax.all_gather(values_own, "blk", axis=0, tiled=True),
+        plate_manage(values_own),
     )
     cot_full = lax.all_gather(cotangent, ("heads", "sub"), axis=1, tiled=True)
     grad_att = jnp.dot(cot_full, w_output, preferred_element_type=jnp.float32).astype(jnp.bfloat16)

time: 203 us -> 207 us (1.020)
  blocking collectives: 48.9 us -> 33.6 us
  local copies, waits for them, and re-layouts: 7.87 us -> 12.8 us
  starting transfers between devices: 13.7 us -> 17.8 us
  other arithmetic: 9.88 us -> 13.6 us
  waiting for transfers between devices: 92.5 us -> 95.7 us
  matrix products: 14.4 us -> 17.5 us
    all_gather x1 -> x0, blocking collectives: 14.4 us -> none  [per_device(): lax.all_gather(values_own, 'blk', axis=0, tiled=True)]
    ppermute x0 -> x3, starting transfers between devices: none -> 6.69 us  [the longest x1 4.72 us: plate_manage(): piece_out = lax.ppermute(e_next[-1], along_axis, lanes)]
    ppermute x0 -> x3, waiting for transfers between devices: none -> 4.21 us  [the longest x2 4.21 us: plate_manage(): aux = lax.ppermute(w1[-1], along_axis, seen)]
    ppermute x3, starting transfers between devices: 2.73 us -> 0.11 us  [from_behind(): return lax.ppermute(value, axis, pairs)]
    unnamed x10 -> x19, local copies, waits for them, and re-layouts: 0.03 us -> 2.59 us
    dynamic_slice x0 -> x2, local copies, waits for them, and re-layouts: none -> 2.52 us  [plate_manage(): return jnp.roll(parts_out, (before - n_dev_all // 2) * chunk.shape[0], 0)]
    add x3, other arithmetic: 0.09 us -> 2.19 us  [turn(): return (accum_q + query_add, moved + term)]
  transfers between devices with their start and end apart: 9 -> 12, of which waited for: 5 -> 6; matrix products, arithmetic and copies ran while one was open for 9% -> 11% of each run, Pallas kernels for 0% -> 0%
where the time goes in v1:
time: 207 us; the launch traced here: 206 us
  waiting for transfers between devices  95.7 us (46%)
  blocking collectives  33.6 us (16%)
  starting transfers between devices  17.8 us (9%)
  matrix products  17.5 us (8%)
  between operations  14.5 us (7%)
  other arithmetic  13.6 us (7%)
  local copies, waits for them, and re-layouts  12.8 us (6%)
    reduce_scatter x1, waiting for transfers between devices, per_device(): lax.psum_scatter(stacked, 'blk', scatter_dimension=1, tiled=True) * norm  58.1 us
    ppermute x3, waiting for transfers between devices, from_behind(): return lax.ppermute(value, axis, pairs)  17.7 us
    reduce_scatter x1, waiting for transfers between devices, per_device(): lax.psum_scatter(partial_grad, ('heads', 'sub'), scatter_dimension=1, til...  15.6 us
    all_gather x1, blocking collectives, per_device(): lax.all_gather(keys_own, 'blk', axis=0, tiled=True)  14.3 us
    psum x1, blocking collectives, per_device(): conv_grad = lax.psum(conv_terms, 'blk') * norm  13.3 us
    ppermute x2, starting transfers between devices, padded(): lax.ppermute(tail, axis, [(i, (i + 1) % count) for i in range(ends)])  8.34 us
    all_gather x1, blocking collectives, per_device(): cot_full = lax.all_gather(cotangent, ('heads', 'sub'), axis=1, tiled=True)  6 us
    ppermute x1, starting transfers between devices, plate_manage(): piece_out = lax.ppermute(e_next[-1], along_axis, lanes)  4.72 us
  transfers between devices with their start and end apart: 12, of which 6 were waited for; matrix products, arithmetic and copies ran while one was open for 11% of the time, Pallas kernels for 0%

profile of v1, /device:TPU:0, one launch (start us, length us, event | category | flops | bytes accessed | tf_op | source)
XLA Modules:
  0.0 205.7 jit_solution(17939998910977129962)
XLA Ops:
  8.1 4.9 %collective-permute-start.1 = (bf16[1,1024]{1,0:T(2,128)(2,1)S(1)}, bf16[1,1024]{1,0:T(2,128)(2,1)S(1)}, u32[]{:S(2)}, u32[]{:S(2)}) collective-permute-start(bf16[1,1024]{1,0:T(2,128)(2,1)S(1)} %get-tuple-element.416), channel_id=1, source_target_pairs={{0,4},{4,8},{8,12},{1,5},{5,9},{9,13},{2,6},{6,10},{10,14},{3,7},{... | collective-permute-start | bytes 6152 | tf_op jit(solution)/shard_map/ppermute | solution.py:35
  13.0 1.3 collective-permute-start.2
  15.9 6.0 %all_gather.7 = bf16[128,1024]{1,0:T(8,128)(2,1)S(1)} all-gather(bf16[128,256]{1,0:T(8,128)(2,1)} %param.17), channel_id=1, replica_groups=mesh['groups'=2,'blk'=4,'heads'=2,'sub'=2] {'heads','sub'}, dimensions={1}, use_global_device_ids=true | all-gather | bytes 327680 | tf_op jit(solution)/shard_map/all_gather | solution.py:86
  22.2 1.0 convolution_compare_fusion.1
  23.1 1.3 convolution_convert_fusion.2
  24.8 1.0 maximum_convert_fusion
  26.3 4.7 %collective-permute-start.5 = (bf16[128,256]{1,0:T(8,128)(2,1)S(1)}, bf16[128,256]{1,0:T(8,128)(2,1)}, u32[]{:S(2)}, u32[]{:S(2)}) collective-permute-start(bf16[128,256]{1,0:T(8,128)(2,1)S(1)} %convolution_convert_fusion.1), channel_id=1, source_target_pairs={{0,12},{4,0},{8,4},{12,8},{1,13},{5,1},{9,5},{13,9},{2,14},{6,2},{... | collective-permute-start | bytes 196616 | tf_op jit(solution)/shard_map/ppermute | solution.py:20
  31.3 14.3 %all_gather.6 = bf16[512,256]{1,0:T(8,128)(2,1)S(1)} all-gather(bf16[128,256]{1,0:T(8,128)(2,1)S(1)} %convolution_convert_fusion.4), channel_id=1, replica_groups=mesh['groups'=2,'blk'=4,'heads'=2,'sub'=2] {'blk'}, dimensions={0}, use_global_device_ids=true | all-gather | bytes 327680 | tf_op jit(solution)/shard_map/all_gather | solution.py:83
  46.3 2.2 %fusion.50 = (f32[4,128]{1,0:T(4,128)S(1)}, bf16[4,128,512]{2,1,0:T(8,128)(2,1)}) fusion(bf16[128,4,64]{0,2,1:T(8,128)(2,1)S(1)} %bitcast.177, bf16[512,4,64]{0,2,1:T(8,128)(2,1)S(1)} %bitcast.181, pred[128,512]{1,0:T(8,128)(4,1)} %convolution_compare_fusion.1), kind=kOutput, calls=%fused_computation.135 | convolution fusion | flops 34864640 | bytes 919552 | tf_op jit(solution)/shard_map/while/body/eval_jaxpr/qhd,khd->hqk/dot_general | solution.py:102
  48.7 2.0 collective-permute-start.4
  50.8 4.2 %collective-permute-done.4 = bf16[128,256]{1,0:T(8,128)(2,1)S(1)} collective-permute-done((bf16[128,256]{1,0:T(8,128)(2,1)}, bf16[128,256]{1,0:T(8,128)(2,1)S(1)}, u32[]{:S(2)}, u32[]{:S(2)}) %collective-permute-start.4) | collective-permute-done | bytes 65568 | tf_op jit(solution)/shard_map/ppermute | solution.py:17
  59.2 1.8 copy.40
  61.7 2.1 %fusion.37 = (f32[4,128]{1,0:T(4,128)S(1)}, f32[4,128,64]{1,2,0:T(8,128)}) fusion(f32[4,128]{1,0:T(4,128)S(1)} %get-tuple-element.518, bf16[128,256]{0,1:T(8,128)(2,1)S(1)} %copy.38, bf16[512,4,64]{0,2,1:T(8,128)(2,1)} %bitcast.20, bf16[4,128,512]{2,1,0:T(8,128)(2,1)} %get-tuple-element.428), kind=kOutput, calls=%fused_computation.89 | convolution fusion | flops 33684992 | bytes 987136 | tf_op jit(solution)/shard_map/while/body/eval_jaxpr/hqk,khd->hqd/dot_general | solution.py:112
  63.8 1.1 fusion.24
  64.9 1.0 convolution_bitcast_fusion.5
  66.8 27.3 %while.23 = (s32[]{:T(128)}, f32[128,4,64]{0,2,1:T(8,128)S(1)}, f32[2,128,256]{1,2,0:T(8,128)}, s32[]{:T(128)}, bf16[512,256]{0,1:T(8,128)(2,1)S(1)}, /*index=5*...) while((s32[]{:T(128)}, f32[128,4,64]{0,2,1:T(8,128)S(1)}, ...), condition=%wide.region_2.3_spmd, body=%wide.region_1.2_spmd.sunk | while | flops 42853904 | bytes 4331956 | solution.py:173
  69.3 5.8 %collective-permute-done = f32[2,128,256]{1,2,0:T(8,128)S(1)} collective-permute-done((f32[2,128,256]{1,2,0:T(8,128)}, f32[2,128,256]{1,2,0:T(8,128)S(1)}, u32[]{:S(2)}, u32[]{:S(2)}) %collective-permute-start) | collective-permute-done | bytes 262176 | tf_op jit(solution)/shard_map/while/body/eval_jaxpr/ppermute | solution.py:47
  78.3 5.9 %collective-permute-done = f32[2,128,256]{1,2,0:T(8,128)S(1)} collective-permute-done((f32[2,128,256]{1,2,0:T(8,128)}, f32[2,128,256]{1,2,0:T(8,128)S(1)}, u32[]{:S(2)}, u32[]{:S(2)}) %collective-permute-start) | collective-permute-done | bytes 262176 | tf_op jit(solution)/shard_map/while/body/eval_jaxpr/ppermute | solution.py:47
  87.5 5.9 %collective-permute-done = f32[2,128,256]{1,2,0:T(8,128)S(1)} collective-permute-done((f32[2,128,256]{1,2,0:T(8,128)}, f32[2,128,256]{1,2,0:T(8,128)S(1)}, u32[]{:S(2)}, u32[]{:S(2)}) %collective-permute-start) | collective-permute-done | bytes 262176 | tf_op jit(solution)/shard_map/while/body/eval_jaxpr/ppermute | solution.py:47
  94.1 1.0 convert.4
  95.8 1.1 convolution_add_fusion
  98.3 2.2 %pad_maximum_fusion = f32[4,1024,256]{2,1,0:T(8,128)} fusion(f32[1,1024,256]{2,1,0:T(8,128)S(1)} %convolution_bitcast_fusion.1, f32[1,1024,256]{2,1,0:T(8,128)S(1)} %convolution_bitcast_fusion.2, f32[1,1024,256]{2,1,0:T(8,128)S(1)} %convolution_bitcast_fusion.3, f32[1,1024,256]{2,1,0:T(8,128)S(1)} %convolution_bitcast_fusion.4), kind=kLoop, calls=%fused_computation.32 | loop fusion | flops 3145728 | bytes 8388608 | tf_op jit(solution)/shard_map/stack | solution.py:177
  100.6 0.9 dynamic-slice_add_fusion
  101.5 15.6 %reduce-scatter.3.cloned.1.call-done = f32[128,256]{1,0:T(8,128)} async-done(((f32[128,1024]{1,0:T(8,128)}), f32[128,256]{1,0:T(8,128)}) %reduce-scatter.3.cloned.1.call-update) | async-done | bytes 131088 | tf_op jit(solution)/shard_map/reduce_scatter | solution.py:191
  117.0 1.1 fusion.33
  118.1 3.4 %collective-permute-start.6 = (bf16[1,256]{1,0:T(2,128)(2,1)S(1)}, bf16[1,256]{1,0:T(2,128)(2,1)S(1)}, u32[]{:S(2)}, u32[]{:S(2)}) collective-permute-start(bf16[1,256]{1,0:T(2,128)(2,1)S(1)} %get-tuple-element.419), channel_id=1, source_target_pairs={{0,4},{4,8},{8,12},{1,5},{5,9},{9,13},{2,6},{6,10},{10,14},{3,7},{... | collective-permute-start | bytes 1544 | tf_op jit(solution)/shard_map/ppermute | solution.py:35
  121.5 1.3 collective-permute-start.7
  122.8 13.3 %psum.7 = f32[3,256]{1,0:T(4,128)S(1)} all-reduce(f32[3,256]{1,0:T(4,128)S(1)} %pad_maximum_fusion.2), channel_id=1, replica_groups=mesh['groups'=2,'blk'=4,'heads'=2,'sub'=2] {'blk'}, use_global_device_ids=true, to_apply=%region_7.8 | all-reduce | flops 768 | bytes 6144 | tf_op jit(solution)/shard_map/psum | solution.py:211
  136.7 1.6 fusion.34
  138.4 58.1 %reduce-scatter.5.cloned.1.call-done = f32[4,256,256]{2,1,0:T(8,128)} async-done(((f32[4,1024,256]{2,1,0:T(8,128)}), f32[4,256,256]{2,1,0:T(8,128)}) %reduce-scatter.5.cloned.1.call-update) | async-done | bytes 1048592 | tf_op jit(solution)/shard_map/reduce_scatter | solution.py:185
  196.5 1.3 broadcast_multiply_fusion
  197.8 1.0 slice_bitcast_fusion
  (103 shorter events, 22.6 us)
Async XLA Ops:
  7.2 38.6 %copy-start = (bf16[1024,256]{1,0:T(8,128)(2,1)S(1)}, bf16[1024,256]{1,0:T(8,128)(2,1)}, u32[]{:S(2)}) copy-start(bf16[1024,256]{1,0:T(8,128)(2,1)} %param.12) | copy-start | bytes 1572868
  7.2 18.9 %copy-start.2 = (bf16[1024,256]{1,0:T(8,128)(2,1)S(1)}, bf16[1024,256]{1,0:T(8,128)(2,1)}, u32[]{:S(2)}) copy-start(bf16[1024,256]{1,0:T(8,128)(2,1)} %param.14) | copy-start | bytes 1572868
  7.2 23.8 %copy-start.1 = (bf16[1024,256]{1,0:T(8,128)(2,1)S(1)}, bf16[1024,256]{1,0:T(8,128)(2,1)}, u32[]{:S(2)}) copy-start(bf16[1024,256]{1,0:T(8,128)(2,1)} %param.13) | copy-start | bytes 1572868
  7.2 109.8 %reduce-scatter.3.cloned.1.call-start = ((), (), s32[]{:S(2)}) async-start(), calls=%async_computation.2 | async-start | bytes 655360 | tf_op jit(solution)/shard_map/reduce_scatter | solution.py:191
  8.1 16.7 %collective-permute-start.1 = (bf16[1,1024]{1,0:T(2,128)(2,1)S(1)}, bf16[1,1024]{1,0:T(2,128)(2,1)S(1)}, u32[]{:S(2)}, u32[]{:S(2)}) collective-permute-start(bf16[1,1024]{1,0:T(2,128)(2,1)S(1)} %get-tuple-element.416), channel_id=1, source_target_pairs={{0,4},{4,8},{8,12},{1,5},{5,9},{9,13},{2,6},{6,10},{10,14},{3,7},{... | collective-permute-start | bytes 6152 | tf_op jit(solution)/shard_map/ppermute | solution.py:35
  13.0 11.8 %collective-permute-start.2 = (bf16[1,1024]{1,0:T(2,128)(2,1)S(1)}, bf16[1,1024]{1,0:T(2,128)(2,1)S(1)}, u32[]{:S(2)}, u32[]{:S(2)}) collective-permute-start(bf16[1,1024]{1,0:T(2,128)(2,1)S(1)} %get-tuple-element.417), channel_id=1, source_target_pairs={{4,0},{8,4},{12,8},{5,1},{9,5},{13,9},{6,2},{10,6},{14,10},{7,3},{... | collective-permute-start | bytes 6152 | tf_op jit(solution)/shard_map/ppermute | solution.py:37
  26.3 29.6 %collective-permute-start.5 = (bf16[128,256]{1,0:T(8,128)(2,1)S(1)}, bf16[128,256]{1,0:T(8,128)(2,1)}, u32[]{:S(2)}, u32[]{:S(2)}) collective-permute-start(bf16[128,256]{1,0:T(8,128)(2,1)S(1)} %convolution_convert_fusion.1), channel_id=1, source_target_pairs={{0,12},{4,0},{8,4},{12,8},{1,13},{5,1},{9,5},{13,9},{2,14},{6,2},{... | collective-permute-start | bytes 196616 | tf_op jit(solution)/shard_map/ppermute | solution.py:20
  31.0 17.7 %collective-permute-start.3 = (bf16[128,256]{1,0:T(8,128)(2,1)S(1)}, bf16[128,256]{1,0:T(8,128)(2,1)}, u32[]{:S(2)}, u32[]{:S(2)}) collective-permute-start(bf16[128,256]{1,0:T(8,128)(2,1)S(1)} %convolution_convert_fusion.1), channel_id=1, source_target_pairs={{0,4},{4,8},{8,12},{12,0},{1,5},{5,9},{9,13},{13,1},{2,6},{6,10},{... | collective-permute-start | bytes 196616 | tf_op jit(solution)/shard_map/ppermute | solution.py:17
  46.2 4.4 %copy-start.4 = (bf16[128,256]{0,1:T(8,128)(2,1)}, bf16[128,256]{0,1:T(8,128)(2,1)S(1)}, u32[]{:S(2)}) copy-start(bf16[128,256]{0,1:T(8,128)(2,1)S(1)} %copy.35) | copy-start | bytes 196612
  48.7 6.3 %collective-permute-start.4 = (bf16[128,256]{1,0:T(8,128)(2,1)}, bf16[128,256]{1,0:T(8,128)(2,1)S(1)}, u32[]{:S(2)}, u32[]{:S(2)}) collective-permute-start(bf16[128,256]{1,0:T(8,128)(2,1)} %collective-permute-done.3), channel_id=1, source_target_pairs={{0,4},{4,8},{8,12},{12,0},{1,5},{5,9},{9,13},{13,1},{2,6},{6,10},{... | collective-permute-start | bytes 196616 | tf_op jit(solution)/shard_map/ppermute | solution.py:17
  66.8 8.4 %collective-permute-start = (f32[2,128,256]{1,2,0:T(8,128)}, f32[2,128,256]{1,2,0:T(8,128)S(1)}, u32[]{:S(2)}, u32[]{:S(2)}) collective-permute-start(f32[2,128,256]{1,2,0:T(8,128)} %get-tuple-element.531), channel_id=1, source_target_pairs={{0,4},{4,8},{8,12},{12,0},{1,5},{5,9},{9,13},{13,1},{2,6},{6,10},{... | collective-permute-start | bytes 786440 | tf_op jit(solution)/shard_map/while/body/eval_jaxpr/ppermute | solution.py:47
  75.9 8.4 %collective-permute-start = (f32[2,128,256]{1,2,0:T(8,128)}, f32[2,128,256]{1,2,0:T(8,128)S(1)}, u32[]{:S(2)}, u32[]{:S(2)}) collective-permute-start(f32[2,128,256]{1,2,0:T(8,128)} %get-tuple-element.531), channel_id=1, source_target_pairs={{0,4},{4,8},{8,12},{12,0},{1,5},{5,9},{9,13},{13,1},{2,6},{6,10},{... | collective-permute-start | bytes 786440 | tf_op jit(solution)/shard_map/while/body/eval_jaxpr/ppermute | solution.py:47
  85.0 8.4 %collective-permute-start = (f32[2,128,256]{1,2,0:T(8,128)}, f32[2,128,256]{1,2,0:T(8,128)S(1)}, u32[]{:S(2)}, u32[]{:S(2)}) collective-permute-start(f32[2,128,256]{1,2,0:T(8,128)} %get-tuple-element.531), channel_id=1, source_target_pairs={{0,4},{4,8},{8,12},{12,0},{1,5},{5,9},{9,13},{13,1},{2,6},{6,10},{... | collective-permute-start | bytes 786440 | tf_op jit(solution)/shard_map/while/body/eval_jaxpr/ppermute | solution.py:47
  95.4 2.5 %copy-start.5 = (f32[4,128,64]{1,2,0:T(8,128)S(1)}, f32[4,128,64]{1,2,0:T(8,128)}, u32[]{:S(2)}) copy-start(f32[4,128,64]{1,2,0:T(8,128)} %get-tuple-element.430) | copy-start | bytes 393220
  96.9 99.6 %reduce-scatter.5.cloned.1.call-start = ((), (), s32[]{:S(2)}) async-start(), calls=%async_computation.3 | async-start | bytes 5242880 | tf_op jit(solution)/shard_map/reduce_scatter | solution.py:185
  100.5 16.5 %copy-start.3 = (bf16[128,256]{1,0:T(8,128)(2,1)S(1)}, bf16[128,256]{1,0:T(8,128)(2,1)}, u32[]{:S(2)}) copy-start(bf16[128,256]{1,0:T(8,128)(2,1)} %param.17) | copy-start | bytes 196612
  118.1 18.6 %collective-permute-start.6 = (bf16[1,256]{1,0:T(2,128)(2,1)S(1)}, bf16[1,256]{1,0:T(2,128)(2,1)S(1)}, u32[]{:S(2)}, u32[]{:S(2)}) collective-permute-start(bf16[1,256]{1,0:T(2,128)(2,1)S(1)} %get-tuple-element.419), channel_id=1, source_target_pairs={{0,4},{4,8},{8,12},{1,5},{5,9},{9,13},{2,6},{6,10},{10,14},{3,7},{... | collective-permute-start | bytes 1544 | tf_op jit(solution)/shard_map/ppermute | solution.py:35
  121.5 15.2 %collective-permute-start.7 = (bf16[1,256]{1,0:T(2,128)(2,1)S(1)}, bf16[1,256]{1,0:T(2,128)(2,1)S(1)}, u32[]{:S(2)}, u32[]{:S(2)}) collective-permute-start(bf16[1,256]{1,0:T(2,128)(2,1)S(1)} %get-tuple-element.420), channel_id=1, source_target_pairs={{4,0},{8,4},{12,8},{5,1},{9,5},{13,9},{6,2},{10,6},{14,10},{7,3},{... | collective-permute-start | bytes 1544 | tf_op jit(solution)/shard_map/ppermute | solution.py:37
Sparse Core Ops, SparseCore 0:
  97.0 19.9 reduce-scatter.2
  119.4 77.0 reduce-scatter.4
